TPU v7x, 32 devices: a whole 2x2x4 slice. The times are simulated.
32 devices in a mesh: section: 2 (over x), expert: 16 (over z, y, core).
Axes of the slice: x: 2, y: 2, z: 4, core: 2. Of those that a mesh axis runs over, the one named last changes fastest.
Arguments:
- hidden_in: bfloat16 [16, 128, 4096], P(None, 'expert'), may hold values from -6 to 6
- norm_gain: float32 [2, 4096], P('section'), may hold values from 0.5 to 2
- routes: int32 [2, 16, 128, 8], P('section', None, 'expert'), may hold values from 0 to 15, all different within a row; in each aligned block of 8 rows (0 to 7, 8 to 15, ..., all dimensions but the last counted through in order) at most 6 rows name the same one
- gate_codes: int32 [2, 16, 128, 8], P('section', None, 'expert'), may hold values from 1 to 255
- w_gate: bfloat16 [2, 16, 4096, 768], P('section', 'expert'), may hold values from -0.09375 to 0.09375
- w_up: bfloat16 [2, 16, 4096, 768], P('section', 'expert'), may hold values from -0.09375 to 0.09375
- w_down: bfloat16 [2, 16, 768, 4096], P('section', 'expert'), may hold values from -0.21875 to 0.21875
Outputs:
- stashed: bfloat16 [2, 16, 128, 4096], P('section', None, 'expert')
Inputs may be any that keep to these rules, and one draw needn't show every extreme that they name: `routes`: each row names 8 different experts. Within each aligned block of 8 rows (the rows of one device for one layer and micro-batch), no expert is named by more than 6 rows, a bound that some block reaches.
All inputs are finite; a program needn't handle non-finite values.
Results may differ from a plain program's by a relative error of at most 0.025.
Values may be sent and summed in bfloat16 or wider, within the bound.
A program may use at most 64 MiB of HBM per device.

v0:
```python
import jax
import jax.numpy as jnp
from jax import lax
from jax.sharding import PartitionSpec as P


def passed_along(value, axis, steps):
    count = lax.axis_size(axis)
    initial, last = (max(0, -steps), min(count, count - steps))
    return lax.ppermute(value, axis, [(source, source + steps) for source in range(initial, last)])


def slot_index(route_block, experts, capacity):
    matches = (route_block[:, :, None] == jnp.arange(experts, dtype=jnp.int32)).astype(jnp.int32)
    flat_hits = matches.reshape(-1, experts)
    earlier = jnp.cumsum(flat_hits, axis=0) - flat_hits
    position = jnp.sum(earlier * flat_hits, axis=1).reshape(route_block.shape)
    return route_block * capacity + position


def expert_block(flat_rows, gate_matrix, up_matrix, down_matrix):
    gate_part = jnp.dot(flat_rows, gate_matrix, preferred_element_type=jnp.float32)
    up_part = jnp.dot(flat_rows, up_matrix, preferred_element_type=jnp.float32)
    activity = (jax.nn.silu(gate_part) * up_part).astype(jnp.bfloat16)
    return jnp.dot(activity, down_matrix, preferred_element_type=jnp.float32).astype(jnp.bfloat16)


def per_device(hidden_in, norm_gain, routes, gate_codes, w_gate, w_up, w_down):
    experts = lax.axis_size("expert")
    sections = lax.axis_size("section")
    micro_count, row_count, width = hidden_in.shape
    top_count = routes.shape[-1]
    capacity = min(row_count, 3 * row_count * top_count // (2 * experts))
    section_id = lax.axis_index("section")
    gain = norm_gain[0]
    gate_matrix = w_gate[0, 0]
    up_matrix = w_up[0, 0]
    down_matrix = w_down[0, 0]

    def tick(tick_index, carry):
        incoming, stash = carry
        micro_id = tick_index - section_id
        active = jnp.logical_and(micro_id >= 0, micro_id < micro_count)
        chosen = jnp.clip(micro_id, 0, micro_count - 1)
        fresh_rows = lax.dynamic_index_in_dim(hidden_in, chosen, 0, keepdims=False)
        layer_in = jnp.where(section_id == 0, fresh_rows, incoming)
        route_block = lax.dynamic_index_in_dim(routes[0], chosen, 0, keepdims=False)
        code_block = lax.dynamic_index_in_dim(gate_codes[0], chosen, 0, keepdims=False)
        floats = layer_in.astype(jnp.float32)
        scale = lax.rsqrt(jnp.mean(floats * floats, axis=-1, keepdims=True) + 1e-06)
        normed = (floats * scale * gain).astype(jnp.bfloat16)
        codes = code_block.astype(jnp.float32)
        weights = codes / jnp.sum(codes, axis=-1, keepdims=True)
        targets = slot_index(route_block, experts, capacity)
        placing = jnp.sum(
            (targets[..., None] == jnp.arange(experts * capacity, dtype=jnp.int32)).astype(
                jnp.bfloat16
            ),
            axis=1,
        )
        outgoing = jnp.dot(placing.T, normed, preferred_element_type=jnp.float32).astype(
            jnp.bfloat16
        )
        outgoing = outgoing.reshape(experts, capacity, width)
        block_rows = lax.all_to_all(outgoing, "expert", split_axis=0, concat_axis=0, tiled=True)
        flat_rows = block_rows.reshape(-1, width)
        output = lax.cond(
            active,
            lambda rows_in: expert_block(rows_in, gate_matrix, up_matrix, down_matrix),
            lambda rows_in: jnp.zeros_like(rows_in),
            flat_rows,
        )
        finished = output.reshape(block_rows.shape)
        returned = lax.all_to_all(
            finished, "expert", split_axis=0, concat_axis=0, tiled=True
        ).reshape(experts * capacity, width)
        picked = returned[targets]
        mixed = jnp.sum(weights[..., None] * picked.astype(jnp.float32), axis=1)
        layer_out = (floats + mixed).astype(jnp.bfloat16)
        previous = lax.dynamic_index_in_dim(stash, chosen, 0, keepdims=False)
        stash = lax.dynamic_update_index_in_dim(
            stash, jnp.where(active, layer_out, previous), chosen, 0
        )
        incoming = passed_along(layer_out, "section", 1)
        return (incoming, stash)

    start = (
        jnp.zeros((row_count, width), jnp.bfloat16),
        jnp.zeros((micro_count, row_count, width), jnp.bfloat16),
    )
    final_carry = lax.fori_loop(0, micro_count + sections - 1, tick, start)
    return final_carry[1][None]


def solution(mesh):
    return jax.shard_map(
        per_device,
        mesh=mesh,
        in_specs=(
            P(None, "expert", None),
            P("section", None),
            P("section", None, "expert", None),
            P("section", None, "expert", None),
            P("section", "expert", None, None),
            P("section", "expert", None, None),
            P("section", "expert", None, None),
        ),
        out_specs=P("section", None, "expert", None),
        check_vma=False,
    )
```

profile of v0, /device:TPU:18, one launch (start us, length us, event | category | flops | bytes accessed | tf_op | source)
XLA Modules:
  0.0 1431.0 jit_solution(6552459803234534719)
XLA Ops:
  1.8 1428.2 %while.17 = (s32[]{:T(128)}, bf16[8,4096]{1,0:T(8,128)(2,1)S(1)}, bf16[16,8,4096]{2,1,0:T(8,128)(2,1)S(1)}, pred[]{:T(512)}, s32[]{:T(128)}, /*index=5*/bf16[16,...) while((s32[]{:T(128)}, bf16[8,4096]{1,0:T(8,128)(2,1)S(1)}, ...), condition=%wide.region_9.10_spmd, body=%wide.region_0.9_spmd.sunk | while | flops 1820697600 | bytes 37468232 | solution.py:91
  12.1 25.2 %all-to-all-done = bf16[16,6,4096]{2,1,0:T(8,128)(2,1)S(1)} async-done(((bf16[16,6,4096]{2,1,0:T(8,128)(2,1)}), bf16[16,6,4096]{2,1,0:T(8,128)(2,1)S(1)}, u32[]{:S(2)}, u32[]{:S(2)}) %all-to-all-start) | async-done | bytes 786464 | tf_op jit(solution)/shard_map/while/body/eval_jaxpr/all_to_all | solution.py:65
  43.6 24.8 %all-to-all-done.1 = bf16[16,6,4096]{2,1,0:T(8,128)(2,1)S(1)} async-done(((bf16[16,6,4096]{2,1,0:T(8,128)(2,1)}), bf16[16,6,4096]{2,1,0:T(8,128)(2,1)S(1)}, u32[]{:S(2)}, u32[]{:S(2)}) %all-to-all-start.1) | async-done | bytes 786464 | tf_op jit(solution)/shard_map/while/body/eval_jaxpr/all_to_all | solution.py:74
  94.3 25.2 %all-to-all-done = bf16[16,6,4096]{2,1,0:T(8,128)(2,1)S(1)} async-done(((bf16[16,6,4096]{2,1,0:T(8,128)(2,1)}), bf16[16,6,4096]{2,1,0:T(8,128)(2,1)S(1)}, u32[]{:S(2)}, u32[]{:S(2)}) %all-to-all-start) | async-done | bytes 786464 | tf_op jit(solution)/shard_map/while/body/eval_jaxpr/all_to_all | solution.py:65
  137.0 24.8 %all-to-all-done.1 = bf16[16,6,4096]{2,1,0:T(8,128)(2,1)S(1)} async-done(((bf16[16,6,4096]{2,1,0:T(8,128)(2,1)}), bf16[16,6,4096]{2,1,0:T(8,128)(2,1)S(1)}, u32[]{:S(2)}, u32[]{:S(2)}) %all-to-all-start.1) | async-done | bytes 786464 | tf_op jit(solution)/shard_map/while/body/eval_jaxpr/all_to_all | solution.py:74
  178.3 25.2 %all-to-all-done = bf16[16,6,4096]{2,1,0:T(8,128)(2,1)S(1)} async-done(((bf16[16,6,4096]{2,1,0:T(8,128)(2,1)}), bf16[16,6,4096]{2,1,0:T(8,128)(2,1)S(1)}, u32[]{:S(2)}, u32[]{:S(2)}) %all-to-all-start) | async-done | bytes 786464 | tf_op jit(solution)/shard_map/while/body/eval_jaxpr/all_to_all | solution.py:65
  221.1 24.8 %all-to-all-done.1 = bf16[16,6,4096]{2,1,0:T(8,128)(2,1)S(1)} async-done(((bf16[16,6,4096]{2,1,0:T(8,128)(2,1)}), bf16[16,6,4096]{2,1,0:T(8,128)(2,1)S(1)}, u32[]{:S(2)}, u32[]{:S(2)}) %all-to-all-start.1) | async-done | bytes 786464 | tf_op jit(solution)/shard_map/while/body/eval_jaxpr/all_to_all | solution.py:74
  262.3 25.2 %all-to-all-done = bf16[16,6,4096]{2,1,0:T(8,128)(2,1)S(1)} async-done(((bf16[16,6,4096]{2,1,0:T(8,128)(2,1)}), bf16[16,6,4096]{2,1,0:T(8,128)(2,1)S(1)}, u32[]{:S(2)}, u32[]{:S(2)}) %all-to-all-start) | async-done | bytes 786464 | tf_op jit(solution)/shard_map/while/body/eval_jaxpr/all_to_all | solution.py:65
  305.1 24.8 %all-to-all-done.1 = bf16[16,6,4096]{2,1,0:T(8,128)(2,1)S(1)} async-done(((bf16[16,6,4096]{2,1,0:T(8,128)(2,1)}), bf16[16,6,4096]{2,1,0:T(8,128)(2,1)S(1)}, u32[]{:S(2)}, u32[]{:S(2)}) %all-to-all-start.1) | async-done | bytes 786464 | tf_op jit(solution)/shard_map/while/body/eval_jaxpr/all_to_all | solution.py:74
  346.3 25.2 %all-to-all-done = bf16[16,6,4096]{2,1,0:T(8,128)(2,1)S(1)} async-done(((bf16[16,6,4096]{2,1,0:T(8,128)(2,1)}), bf16[16,6,4096]{2,1,0:T(8,128)(2,1)S(1)}, u32[]{:S(2)}, u32[]{:S(2)}) %all-to-all-start) | async-done | bytes 786464 | tf_op jit(solution)/shard_map/while/body/eval_jaxpr/all_to_all | solution.py:65
  389.1 24.8 %all-to-all-done.1 = bf16[16,6,4096]{2,1,0:T(8,128)(2,1)S(1)} async-done(((bf16[16,6,4096]{2,1,0:T(8,128)(2,1)}), bf16[16,6,4096]{2,1,0:T(8,128)(2,1)S(1)}, u32[]{:S(2)}, u32[]{:S(2)}) %all-to-all-start.1) | async-done | bytes 786464 | tf_op jit(solution)/shard_map/while/body/eval_jaxpr/all_to_all | solution.py:74
  430.4 25.2 %all-to-all-done = bf16[16,6,4096]{2,1,0:T(8,128)(2,1)S(1)} async-done(((bf16[16,6,4096]{2,1,0:T(8,128)(2,1)}), bf16[16,6,4096]{2,1,0:T(8,128)(2,1)S(1)}, u32[]{:S(2)}, u32[]{:S(2)}) %all-to-all-start) | async-done | bytes 786464 | tf_op jit(solution)/shard_map/while/body/eval_jaxpr/all_to_all | solution.py:65
  473.1 24.8 %all-to-all-done.1 = bf16[16,6,4096]{2,1,0:T(8,128)(2,1)S(1)} async-done(((bf16[16,6,4096]{2,1,0:T(8,128)(2,1)}), bf16[16,6,4096]{2,1,0:T(8,128)(2,1)S(1)}, u32[]{:S(2)}, u32[]{:S(2)}) %all-to-all-start.1) | async-done | bytes 786464 | tf_op jit(solution)/shard_map/while/body/eval_jaxpr/all_to_all | solution.py:74
  514.4 25.2 %all-to-all-done = bf16[16,6,4096]{2,1,0:T(8,128)(2,1)S(1)} async-done(((bf16[16,6,4096]{2,1,0:T(8,128)(2,1)}), bf16[16,6,4096]{2,1,0:T(8,128)(2,1)S(1)}, u32[]{:S(2)}, u32[]{:S(2)}) %all-to-all-start) | async-done | bytes 786464 | tf_op jit(solution)/shard_map/while/body/eval_jaxpr/all_to_all | solution.py:65
  557.2 24.8 %all-to-all-done.1 = bf16[16,6,4096]{2,1,0:T(8,128)(2,1)S(1)} async-done(((bf16[16,6,4096]{2,1,0:T(8,128)(2,1)}), bf16[16,6,4096]{2,1,0:T(8,128)(2,1)S(1)}, u32[]{:S(2)}, u32[]{:S(2)}) %all-to-all-start.1) | async-done | bytes 786464 | tf_op jit(solution)/shard_map/while/body/eval_jaxpr/all_to_all | solution.py:74
  598.4 25.2 %all-to-all-done = bf16[16,6,4096]{2,1,0:T(8,128)(2,1)S(1)} async-done(((bf16[16,6,4096]{2,1,0:T(8,128)(2,1)}), bf16[16,6,4096]{2,1,0:T(8,128)(2,1)S(1)}, u32[]{:S(2)}, u32[]{:S(2)}) %all-to-all-start) | async-done | bytes 786464 | tf_op jit(solution)/shard_map/while/body/eval_jaxpr/all_to_all | solution.py:65
  641.2 24.8 %all-to-all-done.1 = bf16[16,6,4096]{2,1,0:T(8,128)(2,1)S(1)} async-done(((bf16[16,6,4096]{2,1,0:T(8,128)(2,1)}), bf16[16,6,4096]{2,1,0:T(8,128)(2,1)S(1)}, u32[]{:S(2)}, u32[]{:S(2)}) %all-to-all-start.1) | async-done | bytes 786464 | tf_op jit(solution)/shard_map/while/body/eval_jaxpr/all_to_all | solution.py:74
  682.4 25.2 %all-to-all-done = bf16[16,6,4096]{2,1,0:T(8,128)(2,1)S(1)} async-done(((bf16[16,6,4096]{2,1,0:T(8,128)(2,1)}), bf16[16,6,4096]{2,1,0:T(8,128)(2,1)S(1)}, u32[]{:S(2)}, u32[]{:S(2)}) %all-to-all-start) | async-done | bytes 786464 | tf_op jit(solution)/shard_map/while/body/eval_jaxpr/all_to_all | solution.py:65
  725.2 24.8 %all-to-all-done.1 = bf16[16,6,4096]{2,1,0:T(8,128)(2,1)S(1)} async-done(((bf16[16,6,4096]{2,1,0:T(8,128)(2,1)}), bf16[16,6,4096]{2,1,0:T(8,128)(2,1)S(1)}, u32[]{:S(2)}, u32[]{:S(2)}) %all-to-all-start.1) | async-done | bytes 786464 | tf_op jit(solution)/shard_map/while/body/eval_jaxpr/all_to_all | solution.py:74
  766.5 25.2 %all-to-all-done = bf16[16,6,4096]{2,1,0:T(8,128)(2,1)S(1)} async-done(((bf16[16,6,4096]{2,1,0:T(8,128)(2,1)}), bf16[16,6,4096]{2,1,0:T(8,128)(2,1)S(1)}, u32[]{:S(2)}, u32[]{:S(2)}) %all-to-all-start) | async-done | bytes 786464 | tf_op jit(solution)/shard_map/while/body/eval_jaxpr/all_to_all | solution.py:65
  809.2 24.8 %all-to-all-done.1 = bf16[16,6,4096]{2,1,0:T(8,128)(2,1)S(1)} async-done(((bf16[16,6,4096]{2,1,0:T(8,128)(2,1)}), bf16[16,6,4096]{2,1,0:T(8,128)(2,1)S(1)}, u32[]{:S(2)}, u32[]{:S(2)}) %all-to-all-start.1) | async-done | bytes 786464 | tf_op jit(solution)/shard_map/while/body/eval_jaxpr/all_to_all | solution.py:74
  850.5 25.2 %all-to-all-done = bf16[16,6,4096]{2,1,0:T(8,128)(2,1)S(1)} async-done(((bf16[16,6,4096]{2,1,0:T(8,128)(2,1)}), bf16[16,6,4096]{2,1,0:T(8,128)(2,1)S(1)}, u32[]{:S(2)}, u32[]{:S(2)}) %all-to-all-start) | async-done | bytes 786464 | tf_op jit(solution)/shard_map/while/body/eval_jaxpr/all_to_all | solution.py:65
  893.3 24.8 %all-to-all-done.1 = bf16[16,6,4096]{2,1,0:T(8,128)(2,1)S(1)} async-done(((bf16[16,6,4096]{2,1,0:T(8,128)(2,1)}), bf16[16,6,4096]{2,1,0:T(8,128)(2,1)S(1)}, u32[]{:S(2)}, u32[]{:S(2)}) %all-to-all-start.1) | async-done | bytes 786464 | tf_op jit(solution)/shard_map/while/body/eval_jaxpr/all_to_all | solution.py:74
  934.5 25.2 %all-to-all-done = bf16[16,6,4096]{2,1,0:T(8,128)(2,1)S(1)} async-done(((bf16[16,6,4096]{2,1,0:T(8,128)(2,1)}), bf16[16,6,4096]{2,1,0:T(8,128)(2,1)S(1)}, u32[]{:S(2)}, u32[]{:S(2)}) %all-to-all-start) | async-done | bytes 786464 | tf_op jit(solution)/shard_map/while/body/eval_jaxpr/all_to_all | solution.py:65
  1018.5 25.2 %all-to-all-done = bf16[16,6,4096]{2,1,0:T(8,128)(2,1)S(1)} async-done(((bf16[16,6,4096]{2,1,0:T(8,128)(2,1)}), bf16[16,6,4096]{2,1,0:T(8,128)(2,1)S(1)}, u32[]{:S(2)}, u32[]{:S(2)}) %all-to-all-start) | async-done | bytes 786464 | tf_op jit(solution)/shard_map/while/body/eval_jaxpr/all_to_all | solution.py:65
  1061.3 24.8 %all-to-all-done.1 = bf16[16,6,4096]{2,1,0:T(8,128)(2,1)S(1)} async-done(((bf16[16,6,4096]{2,1,0:T(8,128)(2,1)}), bf16[16,6,4096]{2,1,0:T(8,128)(2,1)S(1)}, u32[]{:S(2)}, u32[]{:S(2)}) %all-to-all-start.1) | async-done | bytes 786464 | tf_op jit(solution)/shard_map/while/body/eval_jaxpr/all_to_all | solution.py:74
  1102.6 25.2 %all-to-all-done = bf16[16,6,4096]{2,1,0:T(8,128)(2,1)S(1)} async-done(((bf16[16,6,4096]{2,1,0:T(8,128)(2,1)}), bf16[16,6,4096]{2,1,0:T(8,128)(2,1)S(1)}, u32[]{:S(2)}, u32[]{:S(2)}) %all-to-all-start) | async-done | bytes 786464 | tf_op jit(solution)/shard_map/while/body/eval_jaxpr/all_to_all | solution.py:65
  1145.3 24.8 %all-to-all-done.1 = bf16[16,6,4096]{2,1,0:T(8,128)(2,1)S(1)} async-done(((bf16[16,6,4096]{2,1,0:T(8,128)(2,1)}), bf16[16,6,4096]{2,1,0:T(8,128)(2,1)S(1)}, u32[]{:S(2)}, u32[]{:S(2)}) %all-to-all-start.1) | async-done | bytes 786464 | tf_op jit(solution)/shard_map/while/body/eval_jaxpr/all_to_all | solution.py:74
  1186.6 25.2 %all-to-all-done = bf16[16,6,4096]{2,1,0:T(8,128)(2,1)S(1)} async-done(((bf16[16,6,4096]{2,1,0:T(8,128)(2,1)}), bf16[16,6,4096]{2,1,0:T(8,128)(2,1)S(1)}, u32[]{:S(2)}, u32[]{:S(2)}) %all-to-all-start) | async-done | bytes 786464 | tf_op jit(solution)/shard_map/while/body/eval_jaxpr/all_to_all | solution.py:65
  1229.4 24.8 %all-to-all-done.1 = bf16[16,6,4096]{2,1,0:T(8,128)(2,1)S(1)} async-done(((bf16[16,6,4096]{2,1,0:T(8,128)(2,1)}), bf16[16,6,4096]{2,1,0:T(8,128)(2,1)S(1)}, u32[]{:S(2)}, u32[]{:S(2)}) %all-to-all-start.1) | async-done | bytes 786464 | tf_op jit(solution)/shard_map/while/body/eval_jaxpr/all_to_all | solution.py:74
  1270.6 25.2 %all-to-all-done = bf16[16,6,4096]{2,1,0:T(8,128)(2,1)S(1)} async-done(((bf16[16,6,4096]{2,1,0:T(8,128)(2,1)}), bf16[16,6,4096]{2,1,0:T(8,128)(2,1)S(1)}, u32[]{:S(2)}, u32[]{:S(2)}) %all-to-all-start) | async-done | bytes 786464 | tf_op jit(solution)/shard_map/while/body/eval_jaxpr/all_to_all | solution.py:65
  1354.6 25.2 %all-to-all-done = bf16[16,6,4096]{2,1,0:T(8,128)(2,1)S(1)} async-done(((bf16[16,6,4096]{2,1,0:T(8,128)(2,1)}), bf16[16,6,4096]{2,1,0:T(8,128)(2,1)S(1)}, u32[]{:S(2)}, u32[]{:S(2)}) %all-to-all-start) | async-done | bytes 786464 | tf_op jit(solution)/shard_map/while/body/eval_jaxpr/all_to_all | solution.py:65
  (551 shorter events, 835.7 us)
Async XLA Ops:
  5.9 31.4 %all-to-all-start = ((bf16[16,6,4096]{2,1,0:T(8,128)(2,1)}), bf16[16,6,4096]{2,1,0:T(8,128)(2,1)S(1)}, u32[]{:S(2)}, u32[]{:S(2)}) async-start(bf16[16,6,4096]{2,1,0:T(8,128)(2,1)} %reshape.180), calls=%async_computation | async-start | bytes 2097152 | tf_op jit(solution)/shard_map/while/body/eval_jaxpr/all_to_all | solution.py:65
  38.5 29.8 %all-to-all-start.1 = ((bf16[16,6,4096]{2,1,0:T(8,128)(2,1)}), bf16[16,6,4096]{2,1,0:T(8,128)(2,1)S(1)}, u32[]{:S(2)}, u32[]{:S(2)}) async-start(bf16[16,6,4096]{2,1,0:T(8,128)(2,1)} %reshape.181), calls=%async_computation.1 | async-start | bytes 2097152 | tf_op jit(solution)/shard_map/while/body/eval_jaxpr/all_to_all | solution.py:74
  89.3 30.1 %all-to-all-start = ((bf16[16,6,4096]{2,1,0:T(8,128)(2,1)}), bf16[16,6,4096]{2,1,0:T(8,128)(2,1)S(1)}, u32[]{:S(2)}, u32[]{:S(2)}) async-start(bf16[16,6,4096]{2,1,0:T(8,128)(2,1)} %reshape.180), calls=%async_computation | async-start | bytes 2097152 | tf_op jit(solution)/shard_map/while/body/eval_jaxpr/all_to_all | solution.py:65
  132.0 29.8 %all-to-all-start.1 = ((bf16[16,6,4096]{2,1,0:T(8,128)(2,1)}), bf16[16,6,4096]{2,1,0:T(8,128)(2,1)S(1)}, u32[]{:S(2)}, u32[]{:S(2)}) async-start(bf16[16,6,4096]{2,1,0:T(8,128)(2,1)} %reshape.181), calls=%async_computation.1 | async-start | bytes 2097152 | tf_op jit(solution)/shard_map/while/body/eval_jaxpr/all_to_all | solution.py:74
  173.6 29.8 %all-to-all-start = ((bf16[16,6,4096]{2,1,0:T(8,128)(2,1)}), bf16[16,6,4096]{2,1,0:T(8,128)(2,1)S(1)}, u32[]{:S(2)}, u32[]{:S(2)}) async-start(bf16[16,6,4096]{2,1,0:T(8,128)(2,1)} %reshape.180), calls=%async_computation | async-start | bytes 2097152 | tf_op jit(solution)/shard_map/while/body/eval_jaxpr/all_to_all | solution.py:65
  216.0 29.8 %all-to-all-start.1 = ((bf16[16,6,4096]{2,1,0:T(8,128)(2,1)}), bf16[16,6,4096]{2,1,0:T(8,128)(2,1)S(1)}, u32[]{:S(2)}, u32[]{:S(2)}) async-start(bf16[16,6,4096]{2,1,0:T(8,128)(2,1)} %reshape.181), calls=%async_computation.1 | async-start | bytes 2097152 | tf_op jit(solution)/shard_map/while/body/eval_jaxpr/all_to_all | solution.py:74
  257.6 29.8 %all-to-all-start = ((bf16[16,6,4096]{2,1,0:T(8,128)(2,1)}), bf16[16,6,4096]{2,1,0:T(8,128)(2,1)S(1)}, u32[]{:S(2)}, u32[]{:S(2)}) async-start(bf16[16,6,4096]{2,1,0:T(8,128)(2,1)} %reshape.180), calls=%async_computation | async-start | bytes 2097152 | tf_op jit(solution)/shard_map/while/body/eval_jaxpr/all_to_all | solution.py:65
  300.1 29.8 %all-to-all-start.1 = ((bf16[16,6,4096]{2,1,0:T(8,128)(2,1)}), bf16[16,6,4096]{2,1,0:T(8,128)(2,1)S(1)}, u32[]{:S(2)}, u32[]{:S(2)}) async-start(bf16[16,6,4096]{2,1,0:T(8,128)(2,1)} %reshape.181), calls=%async_computation.1 | async-start | bytes 2097152 | tf_op jit(solution)/shard_map/while/body/eval_jaxpr/all_to_all | solution.py:74
  341.7 29.8 %all-to-all-start = ((bf16[16,6,4096]{2,1,0:T(8,128)(2,1)}), bf16[16,6,4096]{2,1,0:T(8,128)(2,1)S(1)}, u32[]{:S(2)}, u32[]{:S(2)}) async-start(bf16[16,6,4096]{2,1,0:T(8,128)(2,1)} %reshape.180), calls=%async_computation | async-start | bytes 2097152 | tf_op jit(solution)/shard_map/while/body/eval_jaxpr/all_to_all | solution.py:65
  384.1 29.8 %all-to-all-start.1 = ((bf16[16,6,4096]{2,1,0:T(8,128)(2,1)}), bf16[16,6,4096]{2,1,0:T(8,128)(2,1)S(1)}, u32[]{:S(2)}, u32[]{:S(2)}) async-start(bf16[16,6,4096]{2,1,0:T(8,128)(2,1)} %reshape.181), calls=%async_computation.1 | async-start | bytes 2097152 | tf_op jit(solution)/shard_map/while/body/eval_jaxpr/all_to_all | solution.py:74
  425.7 29.8 %all-to-all-start = ((bf16[16,6,4096]{2,1,0:T(8,128)(2,1)}), bf16[16,6,4096]{2,1,0:T(8,128)(2,1)S(1)}, u32[]{:S(2)}, u32[]{:S(2)}) async-start(bf16[16,6,4096]{2,1,0:T(8,128)(2,1)} %reshape.180), calls=%async_computation | async-start | bytes 2097152 | tf_op jit(solution)/shard_map/while/body/eval_jaxpr/all_to_all | solution.py:65
  468.1 29.8 %all-to-all-start.1 = ((bf16[16,6,4096]{2,1,0:T(8,128)(2,1)}), bf16[16,6,4096]{2,1,0:T(8,128)(2,1)S(1)}, u32[]{:S(2)}, u32[]{:S(2)}) async-start(bf16[16,6,4096]{2,1,0:T(8,128)(2,1)} %reshape.181), calls=%async_computation.1 | async-start | bytes 2097152 | tf_op jit(solution)/shard_map/while/body/eval_jaxpr/all_to_all | solution.py:74
  509.7 29.8 %all-to-all-start = ((bf16[16,6,4096]{2,1,0:T(8,128)(2,1)}), bf16[16,6,4096]{2,1,0:T(8,128)(2,1)S(1)}, u32[]{:S(2)}, u32[]{:S(2)}) async-start(bf16[16,6,4096]{2,1,0:T(8,128)(2,1)} %reshape.180), calls=%async_computation | async-start | bytes 2097152 | tf_op jit(solution)/shard_map/while/body/eval_jaxpr/all_to_all | solution.py:65
  552.1 29.8 %all-to-all-start.1 = ((bf16[16,6,4096]{2,1,0:T(8,128)(2,1)}), bf16[16,6,4096]{2,1,0:T(8,128)(2,1)S(1)}, u32[]{:S(2)}, u32[]{:S(2)}) async-start(bf16[16,6,4096]{2,1,0:T(8,128)(2,1)} %reshape.181), calls=%async_computation.1 | async-start | bytes 2097152 | tf_op jit(solution)/shard_map/while/body/eval_jaxpr/all_to_all | solution.py:74
  593.8 29.8 %all-to-all-start = ((bf16[16,6,4096]{2,1,0:T(8,128)(2,1)}), bf16[16,6,4096]{2,1,0:T(8,128)(2,1)S(1)}, u32[]{:S(2)}, u32[]{:S(2)}) async-start(bf16[16,6,4096]{2,1,0:T(8,128)(2,1)} %reshape.180), calls=%async_computation | async-start | bytes 2097152 | tf_op jit(solution)/shard_map/while/body/eval_jaxpr/all_to_all | solution.py:65
  636.2 29.8 %all-to-all-start.1 = ((bf16[16,6,4096]{2,1,0:T(8,128)(2,1)}), bf16[16,6,4096]{2,1,0:T(8,128)(2,1)S(1)}, u32[]{:S(2)}, u32[]{:S(2)}) async-start(bf16[16,6,4096]{2,1,0:T(8,128)(2,1)} %reshape.181), calls=%async_computation.1 | async-start | bytes 2097152 | tf_op jit(solution)/shard_map/while/body/eval_jaxpr/all_to_all | solution.py:74
  677.8 29.8 %all-to-all-start = ((bf16[16,6,4096]{2,1,0:T(8,128)(2,1)}), bf16[16,6,4096]{2,1,0:T(8,128)(2,1)S(1)}, u32[]{:S(2)}, u32[]{:S(2)}) async-start(bf16[16,6,4096]{2,1,0:T(8,128)(2,1)} %reshape.180), calls=%async_computation | async-start | bytes 2097152 | tf_op jit(solution)/shard_map/while/body/eval_jaxpr/all_to_all | solution.py:65
  720.2 29.8 %all-to-all-start.1 = ((bf16[16,6,4096]{2,1,0:T(8,128)(2,1)}), bf16[16,6,4096]{2,1,0:T(8,128)(2,1)S(1)}, u32[]{:S(2)}, u32[]{:S(2)}) async-start(bf16[16,6,4096]{2,1,0:T(8,128)(2,1)} %reshape.181), calls=%async_computation.1 | async-start | bytes 2097152 | tf_op jit(solution)/shard_map/while/body/eval_jaxpr/all_to_all | solution.py:74
  761.8 29.8 %all-to-all-start = ((bf16[16,6,4096]{2,1,0:T(8,128)(2,1)}), bf16[16,6,4096]{2,1,0:T(8,128)(2,1)S(1)}, u32[]{:S(2)}, u32[]{:S(2)}) async-start(bf16[16,6,4096]{2,1,0:T(8,128)(2,1)} %reshape.180), calls=%async_computation | async-start | bytes 2097152 | tf_op jit(solution)/shard_map/while/body/eval_jaxpr/all_to_all | solution.py:65
  804.2 29.8 %all-to-all-start.1 = ((bf16[16,6,4096]{2,1,0:T(8,128)(2,1)}), bf16[16,6,4096]{2,1,0:T(8,128)(2,1)S(1)}, u32[]{:S(2)}, u32[]{:S(2)}) async-start(bf16[16,6,4096]{2,1,0:T(8,128)(2,1)} %reshape.181), calls=%async_computation.1 | async-start | bytes 2097152 | tf_op jit(solution)/shard_map/while/body/eval_jaxpr/all_to_all | solution.py:74
  845.8 29.8 %all-to-all-start = ((bf16[16,6,4096]{2,1,0:T(8,128)(2,1)}), bf16[16,6,4096]{2,1,0:T(8,128)(2,1)S(1)}, u32[]{:S(2)}, u32[]{:S(2)}) async-start(bf16[16,6,4096]{2,1,0:T(8,128)(2,1)} %reshape.180), calls=%async_computation | async-start | bytes 2097152 | tf_op jit(solution)/shard_map/while/body/eval_jaxpr/all_to_all | solution.py:65
  888.2 29.8 %all-to-all-start.1 = ((bf16[16,6,4096]{2,1,0:T(8,128)(2,1)}), bf16[16,6,4096]{2,1,0:T(8,128)(2,1)S(1)}, u32[]{:S(2)}, u32[]{:S(2)}) async-start(bf16[16,6,4096]{2,1,0:T(8,128)(2,1)} %reshape.181), calls=%async_computation.1 | async-start | bytes 2097152 | tf_op jit(solution)/shard_map/while/body/eval_jaxpr/all_to_all | solution.py:74
  929.9 29.8 %all-to-all-start = ((bf16[16,6,4096]{2,1,0:T(8,128)(2,1)}), bf16[16,6,4096]{2,1,0:T(8,128)(2,1)S(1)}, u32[]{:S(2)}, u32[]{:S(2)}) async-start(bf16[16,6,4096]{2,1,0:T(8,128)(2,1)} %reshape.180), calls=%async_computation | async-start | bytes 2097152 | tf_op jit(solution)/shard_map/while/body/eval_jaxpr/all_to_all | solution.py:65
  972.3 29.8 %all-to-all-start.1 = ((bf16[16,6,4096]{2,1,0:T(8,128)(2,1)}), bf16[16,6,4096]{2,1,0:T(8,128)(2,1)S(1)}, u32[]{:S(2)}, u32[]{:S(2)}) async-start(bf16[16,6,4096]{2,1,0:T(8,128)(2,1)} %reshape.181), calls=%async_computation.1 | async-start | bytes 2097152 | tf_op jit(solution)/shard_map/while/body/eval_jaxpr/all_to_all | solution.py:74
  1013.9 29.8 %all-to-all-start = ((bf16[16,6,4096]{2,1,0:T(8,128)(2,1)}), bf16[16,6,4096]{2,1,0:T(8,128)(2,1)S(1)}, u32[]{:S(2)}, u32[]{:S(2)}) async-start(bf16[16,6,4096]{2,1,0:T(8,128)(2,1)} %reshape.180), calls=%async_computation | async-start | bytes 2097152 | tf_op jit(solution)/shard_map/while/body/eval_jaxpr/all_to_all | solution.py:65
  1056.3 29.8 %all-to-all-start.1 = ((bf16[16,6,4096]{2,1,0:T(8,128)(2,1)}), bf16[16,6,4096]{2,1,0:T(8,128)(2,1)S(1)}, u32[]{:S(2)}, u32[]{:S(2)}) async-start(bf16[16,6,4096]{2,1,0:T(8,128)(2,1)} %reshape.181), calls=%async_computation.1 | async-start | bytes 2097152 | tf_op jit(solution)/shard_map/while/body/eval_jaxpr/all_to_all | solution.py:74
  1097.9 29.8 %all-to-all-start = ((bf16[16,6,4096]{2,1,0:T(8,128)(2,1)}), bf16[16,6,4096]{2,1,0:T(8,128)(2,1)S(1)}, u32[]{:S(2)}, u32[]{:S(2)}) async-start(bf16[16,6,4096]{2,1,0:T(8,128)(2,1)} %reshape.180), calls=%async_computation | async-start | bytes 2097152 | tf_op jit(solution)/shard_map/while/body/eval_jaxpr/all_to_all | solution.py:65
  1140.3 29.8 %all-to-all-start.1 = ((bf16[16,6,4096]{2,1,0:T(8,128)(2,1)}), bf16[16,6,4096]{2,1,0:T(8,128)(2,1)S(1)}, u32[]{:S(2)}, u32[]{:S(2)}) async-start(bf16[16,6,4096]{2,1,0:T(8,128)(2,1)} %reshape.181), calls=%async_computation.1 | async-start | bytes 2097152 | tf_op jit(solution)/shard_map/while/body/eval_jaxpr/all_to_all | solution.py:74
  1181.9 29.8 %all-to-all-start = ((bf16[16,6,4096]{2,1,0:T(8,128)(2,1)}), bf16[16,6,4096]{2,1,0:T(8,128)(2,1)S(1)}, u32[]{:S(2)}, u32[]{:S(2)}) async-start(bf16[16,6,4096]{2,1,0:T(8,128)(2,1)} %reshape.180), calls=%async_computation | async-start | bytes 2097152 | tf_op jit(solution)/shard_map/while/body/eval_jaxpr/all_to_all | solution.py:65
  1224.3 29.8 %all-to-all-start.1 = ((bf16[16,6,4096]{2,1,0:T(8,128)(2,1)}), bf16[16,6,4096]{2,1,0:T(8,128)(2,1)S(1)}, u32[]{:S(2)}, u32[]{:S(2)}) async-start(bf16[16,6,4096]{2,1,0:T(8,128)(2,1)} %reshape.181), calls=%async_computation.1 | async-start | bytes 2097152 | tf_op jit(solution)/shard_map/while/body/eval_jaxpr/all_to_all | solution.py:74
  1266.0 29.8 %all-to-all-start = ((bf16[16,6,4096]{2,1,0:T(8,128)(2,1)}), bf16[16,6,4096]{2,1,0:T(8,128)(2,1)S(1)}, u32[]{:S(2)}, u32[]{:S(2)}) async-start(bf16[16,6,4096]{2,1,0:T(8,128)(2,1)} %reshape.180), calls=%async_computation | async-start | bytes 2097152 | tf_op jit(solution)/shard_map/while/body/eval_jaxpr/all_to_all | solution.py:65
  1350.0 29.8 %all-to-all-start = ((bf16[16,6,4096]{2,1,0:T(8,128)(2,1)}), bf16[16,6,4096]{2,1,0:T(8,128)(2,1)S(1)}, u32[]{:S(2)}, u32[]{:S(2)}) async-start(bf16[16,6,4096]{2,1,0:T(8,128)(2,1)} %reshape.180), calls=%async_computation | async-start | bytes 2097152 | tf_op jit(solution)/shard_map/while/body/eval_jaxpr/all_to_all | solution.py:65
  (20 other events, 174.5 us)
where the time goes:
time: 1440 us; the launch traced here: 1430 us
  waiting for transfers between devices  941 us (65%)
  matrix products  196 us (14%)
  starting transfers between devices  182 us (13%)
  local copies, waits for them, and re-layouts  73.6 us (5%)
  other arithmetic  36.6 us (3%)
    all_to_all x17, waiting for transfers between devices, tick(): lax.all_to_all(outgoing, 'expert', split_axis=0, concat_axis=0, tiled=True)  428 us
    all_to_all x17, waiting for transfers between devices, tick(): lax.all_to_all(finished, 'expert', split_axis=0, concat_axis=0, tiled=True)  422 us
    dot_general x16, matrix products, expert_block(): jnp.dot(activity, down_matrix, preferred_element_type=jnp.float32)  114 us
    ppermute x17, waiting for transfers between devices, passed_along(): lax.ppermute(value, axis, [(source, source + steps) for source in range(i...  91.7 us
    all_to_all x17, starting transfers between devices, tick(): lax.all_to_all(outgoing, 'expert', split_axis=0, concat_axis=0, tiled=True)  81.1 us
    all_to_all x17, starting transfers between devices, tick(): lax.all_to_all(finished, 'expert', split_axis=0, concat_axis=0, tiled=True)  78.8 us
    dot_general x16, matrix products, expert_block(): jnp.dot(flat_rows, gate_matrix, preferred_element_type=jnp.float32)  62.6 us
  transfers between devices with their start and end apart: 51, of which 51 were waited for; matrix products, arithmetic and copies ran while one was open for 0% of the time, Pallas kernels for 0%

commit v1 on v0

v1 whole, which is shorter than its diff:
```python
import jax
import jax.numpy as jnp
from jax import lax
from jax.sharding import PartitionSpec as P

GROUP = 2
LAG = 2


def per_device(hidden_in, norm_gain, routes, gate_codes, w_gate, w_up, w_down):
    experts = lax.axis_size("expert")
    sections = lax.axis_size("section")
    micro_count, rows, width = hidden_in.shape
    section_id = lax.axis_index("section")
    me = lax.axis_index("expert")
    gain = norm_gain[0]
    gate_matrix, up_matrix, down_matrix = w_gate[0, 0], w_up[0, 0], w_down[0, 0]
    chunks = micro_count // GROUP

    codes = gate_codes[0].astype(jnp.float32)
    weights = codes / jnp.sum(codes, axis=-1, keepdims=True)
    hits = routes[0][..., None] == jnp.arange(experts, dtype=jnp.int32)
    dense = jnp.sum(jnp.where(hits, weights[..., None], 0.0), axis=2)
    mine = lax.all_to_all(
        dense.transpose(2, 0, 1), "expert", split_axis=0, concat_axis=0, tiled=True
    )
    mine = mine.transpose(1, 0, 2)

    stash = jnp.zeros((micro_count, rows, width), jnp.bfloat16)
    outs = []
    for step in range(chunks + LAG * (sections - 1)):
        chunk = step - LAG * section_id
        active = jnp.logical_and(chunk >= 0, chunk < chunks)
        at = jnp.clip(chunk, 0, chunks - 1) * GROUP
        layer_in = lax.dynamic_slice_in_dim(hidden_in, at, GROUP, 0)
        if step >= LAG:
            incoming = lax.ppermute(
                outs[step - LAG], "section", [(s, s + 1) for s in range(sections - 1)]
            )
            layer_in = jnp.where(section_id == 0, layer_in, incoming)
        floats = layer_in.astype(jnp.float32)
        scale = lax.rsqrt(jnp.mean(floats * floats, axis=-1, keepdims=True) + 1e-06)
        normed = (floats * scale * gain).astype(jnp.bfloat16)
        gathered = lax.all_gather(
            normed.reshape(GROUP * rows, width), "expert", axis=0, tiled=True
        )
        gate_part = jnp.dot(gathered, gate_matrix, preferred_element_type=jnp.float32)
        up_part = jnp.dot(gathered, up_matrix, preferred_element_type=jnp.float32)
        act = (jax.nn.silu(gate_part) * up_part).astype(jnp.bfloat16)
        w = lax.dynamic_slice_in_dim(mine, at, GROUP, 0).transpose(1, 0, 2).reshape(-1, 1)
        part = jnp.dot(act, down_matrix, preferred_element_type=jnp.float32) * w
        mixed = lax.psum_scatter(
            part.astype(jnp.bfloat16), "expert", scatter_dimension=0, tiled=True
        )
        out = (floats + mixed.astype(jnp.float32).reshape(floats.shape)).astype(jnp.bfloat16)
        outs.append(out)
        old = lax.dynamic_slice_in_dim(stash, at, GROUP, 0)
        stash = lax.dynamic_update_slice_in_dim(stash, jnp.where(active, out, old), at, 0)
    return stash[None]


def solution(mesh):
    return jax.shard_map(
        per_device,
        mesh=mesh,
        in_specs=(
            P(None, "expert", None),
            P("section", None),
            P("section", None, "expert", None),
            P("section", None, "expert", None),
            P("section", "expert", None, None),
            P("section", "expert", None, None),
            P("section", "expert", None, None),
        ),
        out_specs=P("section", None, "expert", None),
        check_vma=False,
    )
```

time: 1440 us -> 1130 us (0.78)
  starting transfers between devices: 182 us -> 18.4 us
  local copies, waits for them, and re-layouts: 73.6 us -> 6.28 us
  waiting for transfers between devices: 941 us -> 894 us
  matrix products: 196 us -> 166 us
  other arithmetic: 36.6 us -> 19.8 us
  between operations: 0.03 us -> 14.5 us
    all_to_all x34 -> x1, waiting for transfers between devices: 850 us -> 3.88 us  [per_device(): lax.all_to_all(dense.transpose(2, 0, 1), 'expert', split_axis=0, concat_a...]
    reduce_scatter x0 -> x10, waiting for transfers between devices: none -> 558 us  [per_device(): lax.psum_scatter(part.astype(jnp.bfloat16), 'expert', scatter_dimension=0...]
    all_gather x0 -> x10, waiting for transfers between devices: none -> 307 us  [per_device(): lax.all_gather(normed.reshape(GROUP * rows, width), 'expert', axis=0, til...]
    all_to_all x34 -> x1, starting transfers between devices: 160 us -> 6.18 us  [per_device(): lax.all_to_all(dense.transpose(2, 0, 1), 'expert', split_axis=0, concat_a...]
    ppermute x17 -> x8, waiting for transfers between devices: 91.7 us -> 22.7 us  [per_device(): lax.ppermute(outs[step - LAG], 'section', [(s, s + 1) for s in range(sect...]
    reshape x101 -> x0, local copies, waits for them, and re-layouts: 53.2 us -> none  [the longest x17 21 us: tick(): outgoing = outgoing.reshape(experts, capacity, width)]
    dot_general x49 -> x20, matrix products: 196 us -> 166 us  [the longest x10 112 us: per_device(): part = jnp.dot(act, down_matrix, preferred_element_type=jnp.float32) * w]
    reduce_sum x85 -> x7, other arithmetic: 31.3 us -> 2.98 us  [the longest x5 1.86 us: per_device(): scale = lax.rsqrt(jnp.mean(floats * floats, axis=-1, keepdims=True) + 1e-06)]
  transfers between devices with their start and end apart: 51 -> 29, of which waited for: 51 -> 29; matrix products, arithmetic and copies ran while one was open for 0% -> 16% of each run, Pallas kernels for 0% -> 0%
where the time goes in v1:
time: 1130 us; the launch traced here: 1120 us
  waiting for transfers between devices  894 us (79%)
  matrix products  166 us (15%)
  other arithmetic  19.8 us (2%)
  starting transfers between devices  18.4 us (2%)
  between operations  14.5 us (1%)
    reduce_scatter x10, waiting for transfers between devices, per_device(): lax.psum_scatter(part.astype(jnp.bfloat16), 'expert', scatter_dimension=0...  558 us
    all_gather x10, waiting for transfers between devices, per_device(): lax.all_gather(normed.reshape(GROUP * rows, width), 'expert', axis=0, til...  307 us
    dot_general x10, matrix products, per_device(): part = jnp.dot(act, down_matrix, preferred_element_type=jnp.float32) * w  112 us
    dot_general x10, matrix products, per_device(): jnp.dot(gathered, gate_matrix, preferred_element_type=jnp.float32)  53.8 us
    ppermute x8, waiting for transfers between devices, per_device(): lax.ppermute(outs[step - LAG], 'section', [(s, s + 1) for s in range(sect...  22.7 us
  transfers between devices with their start and end apart: 29, of which 29 were waited for; matrix products, arithmetic and copies ran while one was open for 16% of the time, Pallas kernels for 0%

profile of v1, /device:TPU:18, one launch (start us, length us, event | category | flops | bytes accessed | tf_op | source)
XLA Modules:
  0.0 1118.8 jit_solution(9491824004758853259)
XLA Ops:
  13.9 6.2 all-to-all-start
  25.7 24.7 %all-gather.11.cloned.1.call-done = bf16[256,4096]{1,0:T(8,128)(2,1)} async-done(((bf16[16,4096]{1,0:T(8,128)(2,1)}), bf16[256,4096]{1,0:T(8,128)(2,1)}) %all-gather.11.cloned.1.call-update) | async-done | bytes 2097168 | tf_op jit(solution)/shard_map/all_gather | solution.py:44
  55.6 11.1 fusion.117
  67.1 25.6 %all-gather.13.cloned.1.call-done = bf16[256,4096]{1,0:T(8,128)(2,1)} async-done(((bf16[16,4096]{1,0:T(8,128)(2,1)}), bf16[256,4096]{1,0:T(8,128)(2,1)}) %all-gather.13.cloned.1.call-update) | async-done | bytes 2097168 | tf_op jit(solution)/shard_map/all_gather | solution.py:44
  97.9 11.2 %fusion.114 = bf16[256,4096]{1,0:T(8,128)(2,1)} fusion(bf16[1,1,768,4096]{3,2,1,0:T(8,128)(2,1)} %param.13, f32[256]{0:T(256)S(1)} %mul.397, bf16[256,4096]{1,0:T(8,128)(2,1)} %all-gather.13.cloned.1.call-done, bf16[1,1,4096,768]{3,2,1,0:T(8,128)(2,1)} %param.12, f32[256,768]{1,0:T(8,128)S(1)} %fusion.56), kind=kOutput, calls=%fused_computation.78 | convolution fusion | flops 3224502272 | bytes 17564672 | tf_op jit(solution)/shard_map/dot_general | solution.py:51
  109.7 47.9 %reduce-scatter.11.cloned.1.call-done = bf16[16,4096]{1,0:T(8,128)(2,1)} async-done(((bf16[256,4096]{1,0:T(8,128)(2,1)}), bf16[16,4096]{1,0:T(8,128)(2,1)}) %reduce-scatter.11.cloned.1.call-update) | async-done | bytes 131088 | tf_op jit(solution)/shard_map/reduce_scatter | solution.py:52
  158.6 63.6 %reduce-scatter.13.cloned.1.call-done = bf16[16,4096]{1,0:T(8,128)(2,1)} async-done(((bf16[256,4096]{1,0:T(8,128)(2,1)}), bf16[16,4096]{1,0:T(8,128)(2,1)}) %reduce-scatter.13.cloned.1.call-update) | async-done | bytes 131088 | tf_op jit(solution)/shard_map/reduce_scatter | solution.py:52
  233.4 39.0 %all-gather.15.cloned.1.call-done = bf16[256,4096]{1,0:T(8,128)(2,1)} async-done(((bf16[16,4096]{1,0:T(8,128)(2,1)}), bf16[256,4096]{1,0:T(8,128)(2,1)}) %all-gather.15.cloned.1.call-update) | async-done | bytes 2097168 | tf_op jit(solution)/shard_map/all_gather | solution.py:44
  278.5 11.4 %fusion.111 = bf16[256,4096]{1,0:T(8,128)(2,1)} fusion(bf16[1,1,768,4096]{3,2,1,0:T(8,128)(2,1)} %param.13, f32[256]{0:T(256)S(1)} %mul.407, bf16[256,4096]{1,0:T(8,128)(2,1)} %all-gather.15.cloned.1.call-done, bf16[1,1,4096,768]{3,2,1,0:T(8,128)(2,1)} %param.12, f32[256,768]{1,0:T(8,128)} %fusion.54), kind=kOutput, calls=%fused_computation.77 | convolution fusion | flops 3224502272 | bytes 17564672 | tf_op jit(solution)/shard_map/dot_general | solution.py:51
  290.2 24.4 %all-gather.17.cloned.1.call-done = bf16[256,4096]{1,0:T(8,128)(2,1)} async-done(((bf16[16,4096]{1,0:T(8,128)(2,1)}), bf16[256,4096]{1,0:T(8,128)(2,1)}) %all-gather.17.cloned.1.call-update) | async-done | bytes 2097168 | tf_op jit(solution)/shard_map/all_gather | solution.py:44
  314.6 6.1 fusion.52
  320.7 11.4 %fusion.108 = bf16[256,4096]{1,0:T(8,128)(2,1)} fusion(bf16[1,1,768,4096]{3,2,1,0:T(8,128)(2,1)} %param.13, f32[256]{0:T(256)S(1)} %mul.417, bf16[256,4096]{1,0:T(8,128)(2,1)} %all-gather.17.cloned.1.call-done, bf16[1,1,4096,768]{3,2,1,0:T(8,128)(2,1)} %param.12, f32[256,768]{1,0:T(8,128)} %fusion.52), kind=kOutput, calls=%fused_computation.76 | convolution fusion | flops 3224502272 | bytes 17564672 | tf_op jit(solution)/shard_map/dot_general | solution.py:51
  332.2 47.3 %reduce-scatter.15.cloned.1.call-done = bf16[16,4096]{1,0:T(8,128)(2,1)} async-done(((bf16[256,4096]{1,0:T(8,128)(2,1)}), bf16[16,4096]{1,0:T(8,128)(2,1)}) %reduce-scatter.15.cloned.1.call-update) | async-done | bytes 131088 | tf_op jit(solution)/shard_map/reduce_scatter | solution.py:52
  380.5 63.8 %reduce-scatter.17.cloned.1.call-done = bf16[16,4096]{1,0:T(8,128)(2,1)} async-done(((bf16[256,4096]{1,0:T(8,128)(2,1)}), bf16[16,4096]{1,0:T(8,128)(2,1)}) %reduce-scatter.17.cloned.1.call-update) | async-done | bytes 131088 | tf_op jit(solution)/shard_map/reduce_scatter | solution.py:52
  455.7 38.8 %all-gather.19.cloned.1.call-done = bf16[256,4096]{1,0:T(8,128)(2,1)} async-done(((bf16[16,4096]{1,0:T(8,128)(2,1)}), bf16[256,4096]{1,0:T(8,128)(2,1)}) %all-gather.19.cloned.1.call-update) | async-done | bytes 2097168 | tf_op jit(solution)/shard_map/all_gather | solution.py:44
  499.7 11.1 fusion.105
  511.1 25.6 %all-gather.21.cloned.1.call-done = bf16[256,4096]{1,0:T(8,128)(2,1)} async-done(((bf16[16,4096]{1,0:T(8,128)(2,1)}), bf16[256,4096]{1,0:T(8,128)(2,1)}) %all-gather.21.cloned.1.call-update) | async-done | bytes 2097168 | tf_op jit(solution)/shard_map/all_gather | solution.py:44
  541.9 11.2 fusion.102
  553.1 48.4 %reduce-scatter.19.cloned.1.call-done = bf16[16,4096]{1,0:T(8,128)(2,1)} async-done(((bf16[256,4096]{1,0:T(8,128)(2,1)}), bf16[16,4096]{1,0:T(8,128)(2,1)}) %reduce-scatter.19.cloned.1.call-update) | async-done | bytes 131088 | tf_op jit(solution)/shard_map/reduce_scatter | solution.py:52
  602.5 63.7 %reduce-scatter.21.cloned.1.call-done = bf16[16,4096]{1,0:T(8,128)(2,1)} async-done(((bf16[256,4096]{1,0:T(8,128)(2,1)}), bf16[16,4096]{1,0:T(8,128)(2,1)}) %reduce-scatter.21.cloned.1.call-update) | async-done | bytes 131088 | tf_op jit(solution)/shard_map/reduce_scatter | solution.py:52
  677.6 38.8 %all-gather.23.cloned.1.call-done = bf16[256,4096]{1,0:T(8,128)(2,1)} async-done(((bf16[16,4096]{1,0:T(8,128)(2,1)}), bf16[256,4096]{1,0:T(8,128)(2,1)}) %all-gather.23.cloned.1.call-update) | async-done | bytes 2097168 | tf_op jit(solution)/shard_map/all_gather | solution.py:44
  721.6 11.1 fusion.99
  733.0 25.6 %all-gather.25.cloned.1.call-done = bf16[256,4096]{1,0:T(8,128)(2,1)} async-done(((bf16[16,4096]{1,0:T(8,128)(2,1)}), bf16[256,4096]{1,0:T(8,128)(2,1)}) %all-gather.25.cloned.1.call-update) | async-done | bytes 2097168 | tf_op jit(solution)/shard_map/all_gather | solution.py:44
  763.8 11.2 fusion.96
  775.1 48.2 %reduce-scatter.23.cloned.1.call-done = bf16[16,4096]{1,0:T(8,128)(2,1)} async-done(((bf16[256,4096]{1,0:T(8,128)(2,1)}), bf16[16,4096]{1,0:T(8,128)(2,1)}) %reduce-scatter.23.cloned.1.call-update) | async-done | bytes 131088 | tf_op jit(solution)/shard_map/reduce_scatter | solution.py:52
  824.3 63.7 %reduce-scatter.25.cloned.1.call-done = bf16[16,4096]{1,0:T(8,128)(2,1)} async-done(((bf16[256,4096]{1,0:T(8,128)(2,1)}), bf16[16,4096]{1,0:T(8,128)(2,1)}) %reduce-scatter.25.cloned.1.call-update) | async-done | bytes 131088 | tf_op jit(solution)/shard_map/reduce_scatter | solution.py:52
  899.4 38.7 %all-gather.27.cloned.1.call-done = bf16[256,4096]{1,0:T(8,128)(2,1)} async-done(((bf16[16,4096]{1,0:T(8,128)(2,1)}), bf16[256,4096]{1,0:T(8,128)(2,1)}) %all-gather.27.cloned.1.call-update) | async-done | bytes 2097168 | tf_op jit(solution)/shard_map/all_gather | solution.py:44
  943.4 11.1 fusion.93
  954.8 25.6 %all-gather.29.cloned.1.call-done = bf16[256,4096]{1,0:T(8,128)(2,1)} async-done(((bf16[16,4096]{1,0:T(8,128)(2,1)}), bf16[256,4096]{1,0:T(8,128)(2,1)}) %all-gather.29.cloned.1.call-update) | async-done | bytes 2097168 | tf_op jit(solution)/shard_map/all_gather | solution.py:44
  985.6 11.2 fusion.90
  996.8 48.5 %reduce-scatter.27.cloned.1.call-done = bf16[16,4096]{1,0:T(8,128)(2,1)} async-done(((bf16[256,4096]{1,0:T(8,128)(2,1)}), bf16[16,4096]{1,0:T(8,128)(2,1)}) %reduce-scatter.27.cloned.1.call-update) | async-done | bytes 131088 | tf_op jit(solution)/shard_map/reduce_scatter | solution.py:52
  1047.2 62.7 %reduce-scatter.29.cloned.1.call-done = bf16[16,4096]{1,0:T(8,128)(2,1)} async-done(((bf16[256,4096]{1,0:T(8,128)(2,1)}), bf16[16,4096]{1,0:T(8,128)(2,1)}) %reduce-scatter.29.cloned.1.call-update) | async-done | bytes 131088 | tf_op jit(solution)/shard_map/reduce_scatter | solution.py:52
  (132 shorter events, 115.5 us)
Async XLA Ops:
  6.5 43.8 %all-gather.11.cloned.1.call-start = ((), (), s32[]{:S(2)}) async-start(), calls=%async_computation.11 | async-start | bytes 2228224 | tf_op jit(solution)/shard_map/all_gather | solution.py:44
  9.5 83.2 %all-gather.13.cloned.1.call-start = ((), (), s32[]{:S(2)}) async-start(), calls=%async_computation.13 | async-start | bytes 2228224 | tf_op jit(solution)/shard_map/all_gather | solution.py:44
  13.9 10.1 all-to-all-start
  20.1 137.5 %reduce-scatter.11.cloned.1.call-start = ((), (), s32[]{:S(2)}) async-start(), calls=%async_computation.12 | async-start | bytes 2228224 | tf_op jit(solution)/shard_map/reduce_scatter | solution.py:52
  66.7 155.5 %reduce-scatter.13.cloned.1.call-start = ((), (), s32[]{:S(2)}) async-start(), calls=%async_computation.14 | async-start | bytes 2228224 | tf_op jit(solution)/shard_map/reduce_scatter | solution.py:52
  97.9 59.8 %copy-start = (bf16[16,8,4096]{2,1,0:T(8,128)(2,1)S(1)}, bf16[16,8,4096]{2,1,0:T(8,128)(2,1)}, u32[]{:S(2)}) copy-start(bf16[16,8,4096]{2,1,0:T(8,128)(2,1)} %param.7) | copy-start | bytes 3145732
  109.1 122.5 %copy-start.1 = (f32[1,4096]{1,0:T(1,128)S(1)}, f32[1,4096]{1,0:T(1,128)}, u32[]{:S(2)}) copy-start(f32[1,4096]{1,0:T(1,128)} %param.8) | copy-start | bytes 49156
  109.1 163.3 %all-gather.15.cloned.1.call-start = ((), (), s32[]{:S(2)}) async-start(), calls=%async_computation.15 | async-start | bytes 2228224 | tf_op jit(solution)/shard_map/all_gather | solution.py:44
  223.2 6.9 collective-permute-start.1
  224.5 7.0 collective-permute-start
  232.5 82.1 %all-gather.17.cloned.1.call-start = ((), (), s32[]{:S(2)}) async-start(), calls=%async_computation.17 | async-start | bytes 2228224 | tf_op jit(solution)/shard_map/all_gather | solution.py:44
  233.1 146.4 %reduce-scatter.15.cloned.1.call-start = ((), (), s32[]{:S(2)}) async-start(), calls=%async_computation.16 | async-start | bytes 2228224 | tf_op jit(solution)/shard_map/reduce_scatter | solution.py:52
  289.9 154.4 %reduce-scatter.17.cloned.1.call-start = ((), (), s32[]{:S(2)}) async-start(), calls=%async_computation.18 | async-start | bytes 2228224 | tf_op jit(solution)/shard_map/reduce_scatter | solution.py:52
  332.2 162.3 %all-gather.19.cloned.1.call-start = ((), (), s32[]{:S(2)}) async-start(), calls=%async_computation.19 | async-start | bytes 2228224 | tf_op jit(solution)/shard_map/all_gather | solution.py:44
  445.2 6.9 collective-permute-start.3
  446.5 7.0 collective-permute-start.2
  454.6 82.1 %all-gather.21.cloned.1.call-start = ((), (), s32[]{:S(2)}) async-start(), calls=%async_computation.21 | async-start | bytes 2228224 | tf_op jit(solution)/shard_map/all_gather | solution.py:44
  455.2 146.4 %reduce-scatter.19.cloned.1.call-start = ((), (), s32[]{:S(2)}) async-start(), calls=%async_computation.20 | async-start | bytes 2228224 | tf_op jit(solution)/shard_map/reduce_scatter | solution.py:52
  510.8 155.4 %reduce-scatter.21.cloned.1.call-start = ((), (), s32[]{:S(2)}) async-start(), calls=%async_computation.22 | async-start | bytes 2228224 | tf_op jit(solution)/shard_map/reduce_scatter | solution.py:52
  553.1 163.3 %all-gather.23.cloned.1.call-start = ((), (), s32[]{:S(2)}) async-start(), calls=%async_computation.23 | async-start | bytes 2228224 | tf_op jit(solution)/shard_map/all_gather | solution.py:44
  667.2 6.9 collective-permute-start.5
  668.5 7.0 collective-permute-start.4
  676.5 82.1 %all-gather.25.cloned.1.call-start = ((), (), s32[]{:S(2)}) async-start(), calls=%async_computation.25 | async-start | bytes 2228224 | tf_op jit(solution)/shard_map/all_gather | solution.py:44
  677.1 146.2 %reduce-scatter.23.cloned.1.call-start = ((), (), s32[]{:S(2)}) async-start(), calls=%async_computation.24 | async-start | bytes 2228224 | tf_op jit(solution)/shard_map/reduce_scatter | solution.py:52
  732.7 155.3 %reduce-scatter.25.cloned.1.call-start = ((), (), s32[]{:S(2)}) async-start(), calls=%async_computation.26 | async-start | bytes 2228224 | tf_op jit(solution)/shard_map/reduce_scatter | solution.py:52
  775.0 163.1 %all-gather.27.cloned.1.call-start = ((), (), s32[]{:S(2)}) async-start(), calls=%async_computation.27 | async-start | bytes 2228224 | tf_op jit(solution)/shard_map/all_gather | solution.py:44
  888.9 6.9 collective-permute-start.7
  890.2 7.0 collective-permute-start.6
  898.3 82.1 %all-gather.29.cloned.1.call-start = ((), (), s32[]{:S(2)}) async-start(), calls=%async_computation.29 | async-start | bytes 2228224 | tf_op jit(solution)/shard_map/all_gather | solution.py:44
  898.9 146.4 %reduce-scatter.27.cloned.1.call-start = ((), (), s32[]{:S(2)}) async-start(), calls=%async_computation.28 | async-start | bytes 2228224 | tf_op jit(solution)/shard_map/reduce_scatter | solution.py:52
  954.5 155.4 %reduce-scatter.29.cloned.1.call-start = ((), (), s32[]{:S(2)}) async-start(), calls=%async_computation.30 | async-start | bytes 2228224 | tf_op jit(solution)/shard_map/reduce_scatter | solution.py:52
Sparse Core Ops, SparseCore 0:
  9.6 40.6 all-gather.10
  52.5 40.0 all-gather.12
  96.4 61.1 reduce-scatter.10
  161.6 60.5 reduce-scatter.12
  232.6 39.7 all-gather.14
  274.4 40.1 all-gather.16
  318.3 61.1 reduce-scatter.14
  383.7 60.5 reduce-scatter.16
  454.7 39.7 all-gather.18
  496.5 40.1 all-gather.20
  540.4 61.0 reduce-scatter.18
  605.6 60.5 reduce-scatter.20
  676.6 39.7 all-gather.22
  718.4 40.1 all-gather.24
  762.2 61.0 reduce-scatter.22
  827.4 60.5 reduce-scatter.24
  898.4 39.7 all-gather.26
  940.2 40.1 all-gather.28
  984.1 61.1 reduce-scatter.26
  1049.3 60.5 reduce-scatter.28

commit v2 on v1

v2 whole, which is shorter than its diff:
```python
import functools

import jax
import jax.numpy as jnp
from jax import lax
from jax.experimental import pallas as pl
from jax.experimental.pallas import tpu as pltpu
from jax.sharding import PartitionSpec as P

MESH = pl.DeviceIdType.MESH
ROWS = 16


def moe_kernel(sections, line, hidden, gain, mine, wg, wu, wd, out,
               X, G, A, Pt, RC, RY, RZ, Q,
               x_send, x_recv, az_send, az_recv, ay_send, ay_recv, ac_send, ac_recv,
               rc_send, rc_recv, ry_send, ry_recv, rz_send, rz_recv):
    chunks, _, width = hidden.shape
    hid = wg.shape[1]
    s = lax.axis_index("section")
    e = lax.axis_index("expert")
    c = lax.rem(e, 2)
    y = lax.rem(e // 2, 2)
    z = e // 4

    def dev(zz, yy, cc):
        return (s, (zz * 2 + yy) * 2 + cc)

    sibling = dev(z, y, 1 - c)
    across = dev(z, 1 - y, c)
    others = [dev(lax.rem(z + i, line), y, c) for i in range(1, line)]
    here = y * line + z

    barrier = pltpu.get_barrier_semaphore()
    for d in [sibling, across] + others:
        pl.semaphore_signal(barrier, inc=1, device_id=d, device_id_type=MESH)

    @pl.when(s > 0)
    def _():
        pl.semaphore_signal(barrier, inc=1, device_id=(s - 1, e), device_id_type=MESH)

    @pl.when(s < sections - 1)
    def _():
        pl.semaphore_signal(barrier, inc=1, device_id=(s + 1, e), device_id_type=MESH)

    first = (s == 0).astype(jnp.int32)
    last = (s == sections - 1).astype(jnp.int32)
    pl.semaphore_wait(barrier, line + 3 - first - last)

    def remote(src, dst, send, recv, device):
        return pltpu.make_async_remote_copy(
            src_ref=src, dst_ref=dst, send_sem=send, recv_sem=recv,
            device_id=device, device_id_type=MESH)

    def az(k):
        a = lax.rem(k, 3)
        return [remote(G.at[a, c, here], G.at[a, c, here], az_send.at[a, i], az_recv.at[a, i], others[i])
                for i in range(line - 1)]

    def ay(k):
        a = lax.rem(k, 3)
        half = pl.ds(y * line, line)
        return remote(G.at[a, c, half], G.at[a, c, half], ay_send.at[a], ay_recv.at[a], across)

    def ac(k):
        a = lax.rem(k, 3)
        return remote(G.at[a, c], G.at[a, c], ac_send.at[a], ac_recv.at[a], sibling)

    def rc(k):
        b = lax.rem(k, 2)
        return remote(Pt.at[1 - c], RC.at[b], rc_send.at[b], rc_recv.at[b], sibling)

    def ry(k):
        b = lax.rem(k, 2)
        return remote(Q.at[pl.ds((1 - y) * line, line)], RY.at[b], ry_send.at[b], ry_recv.at[b], across)

    def rz(k):
        b = lax.rem(k, 2)
        return [remote(Q.at[y * line + lax.rem(z + i, line)], RZ.at[b, i - 1],
                       rz_send.at[b, i - 1], rz_recv.at[b, i - 1], others[i - 1])
                for i in range(1, line)]

    def xs(r):
        return remote(out.at[r], X.at[r], x_send, x_recv.at[r], (s + 1, e))

    def step(k, carry):
        gather = k < chunks
        work = jnp.logical_and(k >= 1, k <= chunks)
        back = k >= 2
        r = k - 2
        b = lax.rem(k, 2)

        @pl.when(back)
        def _():
            rc(k).start()

        @pl.when(gather)
        def _():
            @pl.when(s == 0)
            def _():
                X[k] = hidden[k]

            @pl.when(s > 0)
            def _():
                remote(out.at[k], X.at[k], x_send, x_recv.at[k], (s - 1, e)).wait_recv()

            v = X[k].astype(jnp.float32)
            scale = lax.rsqrt(jnp.mean(v * v, axis=-1, keepdims=True) + 1e-06)
            G[lax.rem(k, 3), c, here] = (v * scale * gain[...]).astype(jnp.bfloat16)
            for copy in az(k):
                copy.start()

        @pl.when(back)
        def _():
            rc(k).wait()

            def add(i, carry):
                Q[i] = (Pt[c, i].astype(jnp.float32) + RC[b, i].astype(jnp.float32)).astype(jnp.bfloat16)
                return carry

            lax.fori_loop((1 - y) * line, (1 - y) * line + line, add, 0)
            ry(k).start()
            lax.fori_loop(y * line, y * line + line, add, 0)

        @pl.when(work)
        def _():
            def up(j, carry):
                cols = pl.ds(pl.multiple_of(j * 256, 256), 256)
                rows = G[lax.rem(k - 1, 3)].reshape(-1, width)
                g = jnp.dot(rows, wg[:, cols], preferred_element_type=jnp.float32)
                u = jnp.dot(rows, wu[:, cols], preferred_element_type=jnp.float32)
                A[:, cols] = (g / (1.0 + jnp.exp(-g)) * u).astype(jnp.bfloat16)
                return carry

            lax.fori_loop(0, hid // 256, up, 0)

        @pl.when(gather)
        def _():
            for copy in az(k):
                copy.wait()
            ay(k).start()

        @pl.when(back)
        def _():
            ry(k).wait()

            def add(i, carry):
                j = y * line + i
                Q[j] = (Q[j].astype(jnp.float32) + RY[b, i].astype(jnp.float32)).astype(jnp.bfloat16)
                return carry

            lax.fori_loop(0, line, add, 0)
            for copy in rz(k):
                copy.start()

        @pl.when(work)
        def _():
            def down(j, carry):
                cols = pl.ds(pl.multiple_of(j * 256, 256), 256)
                p = jnp.dot(A[...], wd[:, cols], preferred_element_type=jnp.float32) * mine[k - 1]
                Pt[:, :, :, cols] = p.astype(jnp.bfloat16).reshape(2, 2 * line, ROWS, 256)
                return carry

            lax.fori_loop(0, width // 256, down, 0)

        @pl.when(gather)
        def _():
            ay(k).wait()
            ac(k).start()

        @pl.when(back)
        def _():
            for copy in rz(k):
                copy.wait()
            total = Q[here].astype(jnp.float32)
            for i in range(line - 1):
                total = total + RZ[b, i].astype(jnp.float32)
            out[r] = (X[r].astype(jnp.float32) + total).astype(jnp.bfloat16)

            @pl.when(s < sections - 1)
            def _():
                xs(r).start()

        @pl.when(gather)
        def _():
            ac(k).wait()

        @pl.when(jnp.logical_and(back, s < sections - 1))
        def _():
            xs(r).wait_send()

        return carry

    lax.fori_loop(0, chunks + 2, step, 0)


def per_device(hidden_in, norm_gain, routes, gate_codes, w_gate, w_up, w_down):
    experts = lax.axis_size("expert")
    sections = lax.axis_size("section")
    micro_count, rows, width = hidden_in.shape
    line = experts // 4
    group = ROWS // rows
    chunks = micro_count // group
    hid = w_gate.shape[-1]

    codes = gate_codes[0].astype(jnp.float32)
    weights = codes / jnp.sum(codes, axis=-1, keepdims=True)
    hits = routes[0][..., None] == jnp.arange(experts, dtype=jnp.int32)
    dense = jnp.sum(jnp.where(hits, weights[..., None], 0.0), axis=2)
    mine = lax.all_to_all(
        dense.transpose(2, 0, 1), "expert", split_axis=0, concat_axis=0, tiled=True
    )
    mine = mine.reshape(line, 2, 2, chunks, ROWS).transpose(3, 2, 1, 0, 4)
    mine = mine.reshape(chunks, experts * ROWS, 1)

    bf = jnp.bfloat16
    dma = pltpu.SemaphoreType.DMA
    out = pl.pallas_call(
        functools.partial(moe_kernel, sections, line),
        out_shape=jax.ShapeDtypeStruct((chunks, ROWS, width), bf),
        in_specs=[pl.BlockSpec(memory_space=pltpu.VMEM)] * 6,
        out_specs=pl.BlockSpec(memory_space=pltpu.VMEM),
        scratch_shapes=[
            pltpu.VMEM((chunks, ROWS, width), bf),
            pltpu.VMEM((3, 2, 2 * line, ROWS, width), bf),
            pltpu.VMEM((experts * ROWS, hid), bf),
            pltpu.VMEM((2, 2 * line, ROWS, width), bf),
            pltpu.VMEM((2, 2 * line, ROWS, width), bf),
            pltpu.VMEM((2, line, ROWS, width), bf),
            pltpu.VMEM((2, line - 1, ROWS, width), bf),
            pltpu.VMEM((2 * line, ROWS, width), bf),
            dma, dma((chunks,)),
            dma((3, line - 1)), dma((3, line - 1)),
            dma((3,)), dma((3,)), dma((3,)), dma((3,)),
            dma((2,)), dma((2,)), dma((2,)), dma((2,)),
            dma((2, line - 1)), dma((2, line - 1)),
        ],
        compiler_params=pltpu.CompilerParams(
            collective_id=0, has_side_effects=True, vmem_limit_bytes=56 * 2**20
        ),
        cost_estimate=pl.CostEstimate(
            flops=6 * chunks * experts * ROWS * width * hid,
            bytes_accessed=6 * width * hid, transcendentals=0),
    )(hidden_in.reshape(chunks, ROWS, width), norm_gain, mine, w_gate[0, 0], w_up[0, 0], w_down[0, 0])
    return out.reshape(1, micro_count, rows, width)


def solution(mesh):
    return jax.shard_map(
        per_device,
        mesh=mesh,
        in_specs=(
            P(None, "expert", None),
            P("section", None),
            P("section", None, "expert", None),
            P("section", None, "expert", None),
            P("section", "expert", None, None),
            P("section", "expert", None, None),
            P("section", "expert", None, None),
        ),
        out_specs=P("section", None, "expert", None),
        check_vma=False,
    )
```

time: 1130 us -> 417 us (0.37)
  waiting for transfers between devices: 894 us -> 0 us
  Pallas kernels: 0 us -> 395 us
  matrix products: 166 us -> 0 us
  starting transfers between devices: 18.4 us -> 0 us
  other arithmetic: 19.8 us -> 2.56 us
  between operations: 14.5 us -> 0.09 us
    reduce_scatter x10 -> x0, waiting for transfers between devices: 558 us -> none  [per_device(): lax.psum_scatter(part.astype(jnp.bfloat16), 'expert', scatter_dimension=0...]
    pallas_call x0 -> x1, Pallas kernels: none -> 395 us  [per_device(): pl.pallas_call(functools.partial(moe_kernel, sections, line), out_shape=j...]
    all_gather x10 -> x0, waiting for transfers between devices: 307 us -> none  [per_device(): lax.all_gather(normed.reshape(GROUP * rows, width), 'expert', axis=0, til...]
    dot_general x20 -> x0, matrix products: 166 us -> none  [the longest x10 112 us: per_device(): part = jnp.dot(act, down_matrix, preferred_element_type=jnp.float32) * w]
    ppermute x8 -> x0, waiting for transfers between devices: 22.7 us -> none  [per_device(): lax.ppermute(outs[step - LAG], 'section', [(s, s + 1) for s in range(sect...]
  transfers between devices with their start and end apart: 29 -> 0, of which waited for: 29 -> 0; matrix products, arithmetic and copies ran while one was open for 16% -> 0% of each run, Pallas kernels for 0% -> 0%
where the time goes in v2:
time: 417 us; the launch traced here: 413 us
  Pallas kernels  395 us (95%)
  blocking collectives  10.1 us (2%)
  local copies, waits for them, and re-layouts  5.77 us (1%)
    pallas_call x1, Pallas kernels, per_device(): pl.pallas_call(functools.partial(moe_kernel, sections, line), out_shape=j...  395 us
    all_to_all x1, blocking collectives, per_device(): lax.all_to_all(dense.transpose(2, 0, 1), 'expert', split_axis=0, concat_a...  10.1 us

profile of v2, /device:TPU:18, one launch (start us, length us, event | category | flops | bytes accessed | tf_op | source)
XLA Modules:
  0.0 413.4 jit_solution(16598099530866416431)
XLA Ops:
  0.0 0.8 convert_reduce_fusion
  0.8 0.8 bitcast_divide_fusion
  1.6 0.1 copy.20
  1.6 0.8 copy.19
  2.5 0.3 select_reduce_fusion
  2.8 0.1 copy.21
  2.9 0.1 reshape.26
  3.0 10.1 %all_to_all.5 = f32[16,1,128]{2,1,0:T(1,128)S(1)} all-to-all(f32[16,1,128]{2,1,0:T(1,128)S(1)} %reshape.26), channel_id=1, replica_groups=mesh['section'=2,'expert'=16] {'expert'}, dimensions={0} | all-to-all | bytes 16384 | tf_op jit(solution)/shard_map/all_to_all | solution.py:210
  13.1 0.5 broadcast.5
  13.6 0.7 reduce.1
  14.3 0.1 reshape.27
  14.4 0.1 copy.22
  14.5 0.1 reshape.22
  14.6 1.6 reshape.25.mine
  16.2 394.9 %shard_map.73 = bf16[8,16,4096]{2,1,0:T(8,128)(2,1)} custom-call(bf16[8,16,4096]{2,1,0:T(8,128)(2,1)} %bitcast.21, f32[1,4096]{1,0:T(1,128)} %gain.1, f32[8,256,1]{2,1,0:T(8,128)} %reshape.25.mine, bf16[4096,768]{1,0:T(8,128)(2,1)} %bitcast.18, bf16[4096,768]{1,0:T(8,128)(2,1)} %bitcast.19, bf16[768,4096]{1,0:T(8,128)(2,1)} %bitcast.20), custom_call_target="tpu_custom_call" | custom-call | flops 38654705664 | bytes 18874368 | tf_op jit(solution)/shard_map/pallas_call | solution.py:218
  411.1 2.3 copy.26
  (1 shorter events, 0.0 us)

commit v3 on v2

--- a/solution.py
+++ b/solution.py
@@ -90,10 +90,6 @@
         r = k - 2
         b = lax.rem(k, 2)
 
-        @pl.when(back)
-        def _():
-            rc(k).start()
-
         @pl.when(gather)
         def _():
             @pl.when(s == 0)
@@ -132,6 +128,7 @@
                 A[:, cols] = (g / (1.0 + jnp.exp(-g)) * u).astype(jnp.bfloat16)
                 return carry
 
+            ac(k - 1).wait()
             lax.fori_loop(0, hid // 256, up, 0)
 
         @pl.when(gather)
@@ -162,6 +159,7 @@
                 return carry
 
             lax.fori_loop(0, width // 256, down, 0)
+            rc(k + 1).start()
 
         @pl.when(gather)
         def _():
@@ -180,10 +178,6 @@
             @pl.when(s < sections - 1)
             def _():
                 xs(r).start()
-
-        @pl.when(gather)
-        def _():
-            ac(k).wait()
 
         @pl.when(jnp.logical_and(back, s < sections - 1))
         def _():

time: 417 us -> 356 us (0.85)
  Pallas kernels: 395 us -> 334 us
    pallas_call x1, Pallas kernels: 395 us -> 334 us  [per_device(): pl.pallas_call(functools.partial(moe_kernel, sections, line), out_shape=j...]
where the time goes in v3:
time: 356 us; the launch traced here: 353 us
  Pallas kernels  334 us (94%)
  blocking collectives  10.1 us (3%)
  local copies, waits for them, and re-layouts  5.77 us (2%)
    pallas_call x1, Pallas kernels, per_device(): pl.pallas_call(functools.partial(moe_kernel, sections, line), out_shape=j...  334 us
    all_to_all x1, blocking collectives, per_device(): lax.all_to_all(dense.transpose(2, 0, 1), 'expert', split_axis=0, concat_a...  10.1 us

profile of v3, /device:TPU:18, one launch (start us, length us, event | category | flops | bytes accessed | tf_op | source)
XLA Modules:
  0.0 352.8 jit_solution(8898233311898158385)
XLA Ops:
  0.0 0.8 convert_reduce_fusion
  0.8 0.8 bitcast_divide_fusion
  1.6 0.1 copy.20
  1.6 0.8 copy.19
  2.5 0.3 select_reduce_fusion
  2.8 0.1 copy.21
  2.9 0.1 reshape.26
  3.0 10.1 %all_to_all.5 = f32[16,1,128]{2,1,0:T(1,128)S(1)} all-to-all(f32[16,1,128]{2,1,0:T(1,128)S(1)} %reshape.26), channel_id=1, replica_groups=mesh['section'=2,'expert'=16] {'expert'}, dimensions={0} | all-to-all | bytes 16384 | tf_op jit(solution)/shard_map/all_to_all | solution.py:204
  13.1 0.5 broadcast.5
  13.6 0.7 reduce.1
  14.3 0.1 reshape.27
  14.4 0.1 copy.22
  14.5 0.1 reshape.22
  14.6 1.6 reshape.25.mine
  16.2 334.3 %shard_map.73 = bf16[8,16,4096]{2,1,0:T(8,128)(2,1)} custom-call(bf16[8,16,4096]{2,1,0:T(8,128)(2,1)} %bitcast.21, f32[1,4096]{1,0:T(1,128)} %gain.1, f32[8,256,1]{2,1,0:T(8,128)} %reshape.25.mine, bf16[4096,768]{1,0:T(8,128)(2,1)} %bitcast.18, bf16[4096,768]{1,0:T(8,128)(2,1)} %bitcast.19, bf16[768,4096]{1,0:T(8,128)(2,1)} %bitcast.20), custom_call_target="tpu_custom_call" | custom-call | flops 38654705664 | bytes 18874368 | tf_op jit(solution)/shard_map/pallas_call | solution.py:212
  350.6 2.3 copy.26
  (1 shorter events, 0.0 us)

commit v4 on v3

--- a/solution.py
+++ b/solution.py
@@ -9,9 +9,11 @@
 
 MESH = pl.DeviceIdType.MESH
 ROWS = 16
-
-
-def moe_kernel(sections, line, hidden, gain, mine, wg, wu, wd, out,
+LANES = 128
+
+
+def moe_kernel(sections, line, hidden, gain, codes, wg_hbm, wu_hbm, wd_hbm, out,
+               wg, wu, wd, w_sem,
                X, G, A, Pt, RC, RY, RZ, Q,
                x_send, x_recv, az_send, az_recv, ay_send, ay_recv, ac_send, ac_recv,
                rc_send, rc_recv, ry_send, ry_recv, rz_send, rz_recv):
@@ -52,6 +54,11 @@
             src_ref=src, dst_ref=dst, send_sem=send, recv_sem=recv,
             device_id=device, device_id_type=MESH)
 
+    loads = [pltpu.make_async_copy(src, dst, w_sem.at[i])
+             for i, (src, dst) in enumerate(((wg_hbm, wg), (wu_hbm, wu), (wd_hbm, wd)))]
+    for load in loads:
+        load.start()
+
     def az(k):
         a = lax.rem(k, 3)
         return [remote(G.at[a, c, here], G.at[a, c, here], az_send.at[a, i], az_recv.at[a, i], others[i])
@@ -102,7 +109,8 @@
 
             v = X[k].astype(jnp.float32)
             scale = lax.rsqrt(jnp.mean(v * v, axis=-1, keepdims=True) + 1e-06)
-            G[lax.rem(k, 3), c, here] = (v * scale * gain[...]).astype(jnp.bfloat16)
+            G[lax.rem(k, 3), c, here, :, :width] = (v * scale * gain[...]).astype(jnp.bfloat16)
+            G[lax.rem(k, 3), c, here, :, width:] = codes[k]
             for copy in az(k):
                 copy.start()
 
@@ -122,12 +130,17 @@
         def _():
             def up(j, carry):
                 cols = pl.ds(pl.multiple_of(j * 256, 256), 256)
-                rows = G[lax.rem(k - 1, 3)].reshape(-1, width)
+                rows = G[lax.rem(k - 1, 3), :, :, :, :width].reshape(-1, width)
                 g = jnp.dot(rows, wg[:, cols], preferred_element_type=jnp.float32)
                 u = jnp.dot(rows, wu[:, cols], preferred_element_type=jnp.float32)
                 A[:, cols] = (g / (1.0 + jnp.exp(-g)) * u).astype(jnp.bfloat16)
                 return carry
 
+            @pl.when(k == 1)
+            def _():
+                for load in loads:
+                    load.wait()
+
             ac(k - 1).wait()
             lax.fori_loop(0, hid // 256, up, 0)
 
@@ -152,9 +165,14 @@
 
         @pl.when(work)
         def _():
+            parts = G[lax.rem(k - 1, 3), :, :, :, width:].reshape(-1, LANES).astype(jnp.float32)
+            lane = lax.broadcasted_iota(jnp.int32, parts.shape, 1)
+            own = jnp.sum(jnp.where(lane == e, parts, 0.0), axis=1, keepdims=True)
+            mine = own / jnp.sum(parts, axis=1, keepdims=True)
+
             def down(j, carry):
                 cols = pl.ds(pl.multiple_of(j * 256, 256), 256)
-                p = jnp.dot(A[...], wd[:, cols], preferred_element_type=jnp.float32) * mine[k - 1]
+                p = jnp.dot(A[...], wd[:, cols], preferred_element_type=jnp.float32) * mine
                 Pt[:, :, :, cols] = p.astype(jnp.bfloat16).reshape(2, 2 * line, ROWS, 256)
                 return carry
 
@@ -197,26 +215,22 @@
     chunks = micro_count // group
     hid = w_gate.shape[-1]
 
-    codes = gate_codes[0].astype(jnp.float32)
-    weights = codes / jnp.sum(codes, axis=-1, keepdims=True)
-    hits = routes[0][..., None] == jnp.arange(experts, dtype=jnp.int32)
-    dense = jnp.sum(jnp.where(hits, weights[..., None], 0.0), axis=2)
-    mine = lax.all_to_all(
-        dense.transpose(2, 0, 1), "expert", split_axis=0, concat_axis=0, tiled=True
-    )
-    mine = mine.reshape(line, 2, 2, chunks, ROWS).transpose(3, 2, 1, 0, 4)
-    mine = mine.reshape(chunks, experts * ROWS, 1)
+    hits = routes[0][..., None] == jnp.arange(LANES, dtype=jnp.int32)
+    codes = jnp.sum(jnp.where(hits, gate_codes[0][..., None], 0), axis=2)
+    codes = codes.astype(jnp.bfloat16).reshape(chunks, ROWS, LANES)
 
     bf = jnp.bfloat16
     dma = pltpu.SemaphoreType.DMA
     out = pl.pallas_call(
         functools.partial(moe_kernel, sections, line),
         out_shape=jax.ShapeDtypeStruct((chunks, ROWS, width), bf),
-        in_specs=[pl.BlockSpec(memory_space=pltpu.VMEM)] * 6,
+        in_specs=[pl.BlockSpec(memory_space=pltpu.VMEM)] * 3 + [pl.BlockSpec(memory_space=pl.ANY)] * 3,
         out_specs=pl.BlockSpec(memory_space=pltpu.VMEM),
         scratch_shapes=[
+            pltpu.VMEM((width, hid), bf), pltpu.VMEM((width, hid), bf), pltpu.VMEM((hid, width), bf),
+            dma((3,)),
             pltpu.VMEM((chunks, ROWS, width), bf),
-            pltpu.VMEM((3, 2, 2 * line, ROWS, width), bf),
+            pltpu.VMEM((3, 2, 2 * line, ROWS, width + LANES), bf),
             pltpu.VMEM((experts * ROWS, hid), bf),
             pltpu.VMEM((2, 2 * line, ROWS, width), bf),
             pltpu.VMEM((2, 2 * line, ROWS, width), bf),
@@ -235,7 +249,7 @@
         cost_estimate=pl.CostEstimate(
             flops=6 * chunks * experts * ROWS * width * hid,
             bytes_accessed=6 * width * hid, transcendentals=0),
-    )(hidden_in.reshape(chunks, ROWS, width), norm_gain, mine, w_gate[0, 0], w_up[0, 0], w_down[0, 0])
+    )(hidden_in.reshape(chunks, ROWS, width), norm_gain, codes, w_gate[0, 0], w_up[0, 0], w_down[0, 0])
     return out.reshape(1, micro_count, rows, width)
 
 

time: 356 us -> 337 us (0.947)
  blocking collectives: 10.1 us -> 0 us
  Pallas kernels: 334 us -> 329 us
    all_to_all x1 -> x0, blocking collectives: 10.1 us -> none  [per_device(): lax.all_to_all(dense.transpose(2, 0, 1), 'expert', split_axis=0, concat_a...]
    pallas_call x1, Pallas kernels: 334 us -> 329 us  [per_device(): pl.pallas_call(functools.partial(moe_kernel, sections, line), out_shape=j...]
where the time goes in v4:
time: 337 us; the launch traced here: 334 us
  Pallas kernels  329 us (98%)
  local copies, waits for them, and re-layouts  3.97 us (1%)
    pallas_call x1, Pallas kernels, per_device(): pl.pallas_call(functools.partial(moe_kernel, sections, line), out_shape=j...  329 us

profile of v4, /device:TPU:18, one launch (start us, length us, event | category | flops | bytes accessed | tf_op | source)
XLA Modules:
  0.0 334.5 jit_solution(15663613984301445527)
XLA Ops:
  0.0 0.8 copy.10
  0.8 0.8 copy.11
  1.7 0.3 select_reduce_fusion
  2.1 0.6 convert_element_type.7
  2.7 329.5 %shard_map.73 = bf16[8,16,4096]{2,1,0:T(8,128)(2,1)} custom-call(bf16[8,16,4096]{2,1,0:T(8,128)(2,1)} %bitcast.15, f32[1,4096]{1,0:T(1,128)} %gain.1, bf16[8,16,128]{2,1,0:T(8,128)(2,1)} %bitcast.11, bf16[4096,768]{1,0:T(8,128)(2,1)} %bitcast.12, bf16[4096,768]{1,0:T(8,128)(2,1)} %bitcast.13, bf16[768,4096]{1,0:T(8,128)(2,1)} %bitcast.14), custom_call_target="tpu_custom_call" | custom-call | flops 38654705664 | bytes 18874368 | tf_op jit(solution)/shard_map/pallas_call | solution.py:224
  332.2 2.3 copy.13
